TPU v7x, 32 devices: a whole 2x2x4 slice. The times are simulated.
32 devices in a mesh: head: 2 (over core), vis: 16 (over z, y, x).
Axes of the slice: x: 2, y: 2, z: 4, core: 2. Of those that a mesh axis runs over, the one named last changes fastest.
Arguments:
- queries: bfloat16 [2, 128, 4096], P(None, 'vis', 'head'), may hold values from -24 to 24
- keys: bfloat16 [2, 6400, 1024], P(None, 'vis', 'head'), may hold values from -24 to 24
- values: bfloat16 [2, 6400, 1024], P(None, 'vis', 'head'), may hold values from -6 to 6
- d_out: bfloat16 [2, 128, 4096], P(None, 'vis', 'head'), may hold values from -6 to 6
- q_weight: bfloat16 [4096, 4096], P('vis', 'head'), may hold values from -0.09375 to 0.09375
Outputs:
- d_input: bfloat16 [2, 128, 4096], P(None, 'head', 'vis')
- d_keys: bfloat16 [2, 6400, 1024], P(None, 'vis', 'head')
- d_values: bfloat16 [2, 6400, 1024], P(None, 'vis', 'head')
All inputs are finite; a program needn't handle non-finite values.
Results may differ from a plain program's by a relative error of at most 0.014.
Values may be sent and summed in bfloat16 or wider, within the bound.
A program may use at most 64 MiB of HBM per device.

v0:
```python
import math

import jax
import jax.numpy as jnp
from jax import lax
from jax.sharding import PartitionSpec as P

HQ = 32
KVH = 8
HD = 128


def combined_all(part, axis, combine):
    gathered = jax.tree.map(lambda a: lax.all_gather(a, axis), part)

    def take(source):
        return jax.tree.map(lambda a: lax.dynamic_index_in_dim(a, source, 0, False), gathered)

    return lax.fori_loop(
        1, lax.axis_size(axis), lambda source, state: combine(state, take(source)), take(0)
    )


def split_query(block):
    return block.reshape(block.shape[0], block.shape[1], -1, HQ // KVH, HD)


def split_key(block):
    return block.reshape(block.shape[0], block.shape[1], -1, HD)


def block_scores(query_block, key_block):
    product = jnp.einsum(
        "brkgd,bjkd->bkgrj",
        split_query(query_block),
        split_key(key_block),
        preferred_element_type=jnp.float32,
    )
    return product * HD ** (-0.5)


def grad_products(grad_block, value_block):
    return jnp.einsum(
        "brkgd,bjkd->bkgrj",
        split_query(grad_block),
        split_key(value_block),
        preferred_element_type=jnp.float32,
    )


def local_stats(query_block, grad_block, keys, values):
    scores = block_scores(query_block, keys)
    run_peak = jnp.max(scores, axis=-1)
    weights_exp = jnp.exp(scores - run_peak[..., None])
    run_total = jnp.sum(weights_exp, axis=-1)
    grad_probs = grad_products(grad_block, values)
    run_weighted = jnp.sum(weights_exp * grad_probs, axis=-1)
    return (run_peak, run_total, run_weighted)


def combine_stats(first, second):
    peak_new = jnp.maximum(first[0], second[0])
    scale_first = jnp.exp(first[0] - peak_new)
    scale_second = jnp.exp(second[0] - peak_new)
    total_new = first[1] * scale_first + second[1] * scale_second
    weighted_new = first[2] * scale_first + second[2] * scale_second
    return (peak_new, total_new, weighted_new)


def local_grads(query_block, grad_block, log_part, delta_part, keys, values):
    inv_root = HD ** (-0.5)
    scores = block_scores(query_block, keys)
    probs = jnp.exp(scores - log_part[..., None])
    probs_low = probs.astype(jnp.bfloat16)
    grad_probs = grad_products(grad_block, values)
    grad_low = (probs * (grad_probs - delta_part[..., None])).astype(jnp.bfloat16)
    query_split = split_query(query_block)
    grad_split = split_query(grad_block)
    key_split = split_key(keys)
    batch_size, row_count, query_width = query_block.shape
    batch_size, vis_rows, key_width = keys.shape
    dq_add = (
        jnp.einsum("bkgrj,bjkd->brkgd", grad_low, key_split, preferred_element_type=jnp.float32)
        * inv_root
    )
    key_add = (
        jnp.einsum("bkgrj,brkgd->bjkd", grad_low, query_split, preferred_element_type=jnp.float32)
        * inv_root
    )
    value_add = jnp.einsum(
        "bkgrj,brkgd->bjkd", probs_low, grad_split, preferred_element_type=jnp.float32
    )
    return (
        dq_add.reshape(batch_size, row_count, query_width),
        key_add.reshape(batch_size, vis_rows, key_width),
        value_add.reshape(batch_size, vis_rows, key_width),
    )


def per_device(queries, keys, values, d_out, q_weight):
    batch_size, row_count, query_width = queries.shape
    kv_local = keys.shape[2] // HD
    groups = HQ // KVH
    key_zero = jnp.zeros(keys.shape, jnp.float32)
    whole_query, whole_grad = (
        lax.all_gather(queries, "vis", axis=1, tiled=True),
        lax.all_gather(d_out, "vis", axis=1, tiled=True),
    )
    text_len = whole_query.shape[1]
    block_rows = math.gcd(text_len, 128)
    block_count = text_len // block_rows
    whole_shape = (batch_size, kv_local, groups, text_len)

    def gather_stats(step_index, acc):
        start = step_index * block_rows
        query_block = lax.dynamic_slice_in_dim(whole_query, start, block_rows, 1)
        grad_block = lax.dynamic_slice_in_dim(whole_grad, start, block_rows, 1)
        parts = local_stats(query_block, grad_block, keys, values)
        return tuple(
            (
                lax.dynamic_update_slice_in_dim(held, piece, start, 3)
                for held, piece in zip(acc, parts)
            )
        )

    blank = jnp.zeros(whole_shape, jnp.float32)
    local_all = lax.fori_loop(0, block_count, gather_stats, (blank, blank, blank))
    run_peak, run_total, run_weighted = combined_all(local_all, "vis", combine_stats)
    log_total = run_peak + jnp.log(run_total)
    delta_sum = run_weighted / run_total

    def gather_grads(step_index, acc):
        dq_all, key_acc, value_acc = acc
        start = step_index * block_rows
        query_block = lax.dynamic_slice_in_dim(whole_query, start, block_rows, 1)
        grad_block = lax.dynamic_slice_in_dim(whole_grad, start, block_rows, 1)
        log_block = lax.dynamic_slice_in_dim(log_total, start, block_rows, 3)
        delta_block = lax.dynamic_slice_in_dim(delta_sum, start, block_rows, 3)
        dq_add, key_add, value_add = local_grads(
            query_block, grad_block, log_block, delta_block, keys, values
        )
        dq_all = lax.dynamic_update_slice_in_dim(dq_all, dq_add, start, 1)
        return (dq_all, key_acc + key_add, value_acc + value_add)

    dq_start = jnp.zeros(whole_query.shape, jnp.float32)
    dq_all, key_acc, value_acc = lax.fori_loop(
        0, block_count, gather_grads, (dq_start, key_zero, key_zero)
    )
    dq_home = lax.psum_scatter(dq_all, "vis", scatter_dimension=1, tiled=True)
    dq_low = dq_home.astype(jnp.bfloat16)
    partial_input = jnp.einsum(
        "btq,dq->btd",
        lax.all_gather(dq_low, "vis", axis=1, tiled=True),
        q_weight,
        preferred_element_type=jnp.float32,
    )
    d_input = lax.psum_scatter(
        partial_input.astype(jnp.bfloat16), "head", scatter_dimension=1, tiled=True
    )
    return (d_input, key_acc.astype(jnp.bfloat16), value_acc.astype(jnp.bfloat16))


def solution(mesh):
    placed = (
        P(None, "vis", "head"),
        P(None, "vis", "head"),
        P(None, "vis", "head"),
        P(None, "vis", "head"),
        P("vis", "head"),
    )
    return jax.shard_map(
        per_device,
        mesh=mesh,
        in_specs=placed,
        out_specs=(P(None, "head", "vis"), P(None, "vis", "head"), P(None, "vis", "head")),
        check_vma=False,
    )
```

profile of v0, /device:TPU:0, one launch (start us, length us, event | category | flops | bytes accessed | tf_op | source)
XLA Modules:
  0.0 389.0 jit_solution(7969271115050942384)
XLA Ops:
  7.2 1.6 copy.24
  10.5 1.8 reshape.46
  12.3 2.5 reshape.48
  14.8 54.6 %all-gather.7.cloned.1.call-done = bf16[2,128,2048]{2,0,1:T(2,128)(2,1)} async-done(((bf16[2,8,2048]{2,0,1:T(2,128)(2,1)}), bf16[2,128,2048]{2,0,1:T(2,128)(2,1)}) %all-gather.7.cloned.1.call-update) | async-done | bytes 1048592 | tf_op jit(solution)/shard_map/all_gather | solution.py:106
  69.4 2.5 copy.25
  71.9 3.7 bitcast_reduce_fusion
  75.7 40.2 %all-gather = f32[32,4,4,128]{3,2,1,0:T(4,128)S(1)} all-gather(f32[2,4,4,128]{3,2,1,0:T(4,128)S(1)} %get-tuple-element.264), channel_id=2, replica_groups=mesh['head'=2,'vis'=16] {'vis'}, dimensions={0}, use_global_device_ids=true | all-gather | bytes 278528 | tf_op jit(solution)/shard_map/all_gather | solution.py:14
  115.9 11.3 %all-gather.9.cloned.1.call-done = bf16[2,128,2048]{2,0,1:T(2,128)(2,1)} async-done(((bf16[2,8,2048]{2,0,1:T(2,128)(2,1)}), bf16[2,128,2048]{2,0,1:T(2,128)(2,1)}) %all-gather.9.cloned.1.call-update) | async-done | bytes 1048592 | tf_op jit(solution)/shard_map/all_gather | solution.py:107
  127.2 2.5 copy.29
  129.7 5.8 %fusion.3 = (f32[2,4,4,128]{3,2,1,0:T(4,128)S(1)}, f32[2,4,4,128]{3,2,1,0:T(4,128)S(1)}, f32[2,4,400,128,4]{3,2,4,1,0:T(8,128)}) fusion(f32[2,4,400,128,4]{3,2,4,1,0:T(8,128)} %get-tuple-element.265, f32[2,4,4,128]{3,2,1,0:T(4,128)S(1)} %get-tuple-element.264, bf16[2,128,4,4,128]{1,4,3,2,0:T(8,128)(2,1)S(1)} %bitcast.104, ...), kind=kOutput, calls=%fused_computation.10 | convolution fusion | flops 427614208 | bytes 15024128 | tf_op jit(solution)/shard_map/while/body/eval_jaxpr/brkgd,bjkd->bkgrj/dot_general | solution.py:43
  135.6 40.1 %all-gather.2 = f32[32,4,4,128]{3,2,1,0:T(4,128)S(1)} all-gather(f32[2,4,4,128]{3,2,1,0:T(4,128)S(1)} %get-tuple-element.244), channel_id=4, replica_groups=mesh['head'=2,'vis'=16] {'vis'}, dimensions={0}, use_global_device_ids=true | all-gather | bytes 278528 | tf_op jit(solution)/shard_map/all_gather | solution.py:14
  175.7 36.9 %all-gather.1 = f32[32,4,4,128]{3,2,1,0:T(4,128)S(1)} all-gather(f32[2,4,4,128]{3,2,1,0:T(4,128)S(1)} %get-tuple-element.245), channel_id=3, replica_groups=mesh['head'=2,'vis'=16] {'vis'}, dimensions={0}, use_global_device_ids=true | all-gather | bytes 278528 | tf_op jit(solution)/shard_map/all_gather | solution.py:14
  213.3 12.3 %while.12 = (s32[]{:T(128)}, f32[2,4,4,128]{3,2,1,0:T(4,128)S(1)}, f32[2,4,4,128]{3,2,1,0:T(4,128)S(1)}, f32[2,4,4,128]{3,2,1,0:T(4,128)S(1)}, f32[16,2,4,4,128]...) while((s32[]{:T(128)}, f32[2,4,4,128]{3,2,1,0:T(4,128)S(1)}, ...), condition=%wide.region_4.0_spmd, body=%wide.region_3.4_spmd.sunk | while | flops 45061 | bytes 229519 | solution.py:19
  225.6 6.4 %fusion.5 = bf16[2,4,4,128,400]{3,4,2,1,0:T(8,128)(2,1)S(1)} fusion(f32[2,4,400,128,4]{3,2,4,1,0:T(8,128)} %get-tuple-element.266, f32[2,4,400,128,4]{3,2,4,1,0:T(8,128)} %get-tuple-element.265, f32[2,4,4,128]{3,2,1,0:T(4,128)S(1)} %bitcast.122, f32[2,4,4,128]{3,2,1,0:T(4,128)S(1)} %bitcast.120), kind=kLoop, calls=%fused_computation.12 | loop fusion | flops 8192000 | bytes 16416768 | tf_op jit(solution)/shard_map/while/body/eval_jaxpr/convert_element_type | solution.py:76
  232.0 1.8 copy-done.1
  233.8 2.2 convolution_multiply_fusion
  236.0 2.9 copy.33
  239.0 78.5 %reduce-scatter.3.cloned.1.call-done = f32[2,8,2048]{2,1,0:T(8,128)} async-done(((f32[2,128,2048]{2,1,0:T(8,128)}), f32[2,8,2048]{2,1,0:T(8,128)}) %reduce-scatter.3.cloned.1.call-update) | async-done | bytes 131088 | tf_op jit(solution)/shard_map/reduce_scatter | solution.py:149
  317.5 1.5 convert_element_type.33
  319.1 4.0 %fusion.17 = bf16[2,4,50,8,128]{4,3,2,1,0:T(8,128)(2,1)S(1)} fusion(bf16[2,128,4,4,128]{1,4,3,2,0:T(8,128)(2,1)S(1)} %bitcast.105, f32[2,4,400,128,4]{3,2,4,1,0:T(8,128)} %get-tuple-element.265, f32[2,4,4,128]{3,2,1,0:T(4,128)S(1)} %bitcast.121), kind=kOutput, calls=%fused_computation.27 | convolution fusion | flops 424755200 | bytes 8437760 | tf_op jit(solution)/shard_map/while/body/eval_jaxpr/bkgrj,brkgd->bjkd/dot_general | solution.py:90
  324.2 49.2 %all-gather.11.cloned.1.call-done = bf16[2,128,2048]{2,1,0:T(8,128)(2,1)} async-done(((bf16[2,8,2048]{2,1,0:T(8,128)(2,1)}), bf16[2,128,2048]{2,1,0:T(8,128)(2,1)}) %all-gather.11.cloned.1.call-update) | async-done | bytes 1048592 | tf_op jit(solution)/shard_map/all_gather | solution.py:153
  373.3 2.4 convolution_convert_fusion
  375.7 2.9 fusion.20
  379.7 2.7 reduce-scatter.5.cloned.1.call-done
  (71 shorter events, 16.5 us)
Async XLA Ops:
  7.2 366.2 %copy-start = (bf16[256,2048]{1,0:T(8,128)(2,1)S(1)}, bf16[256,2048]{1,0:T(8,128)(2,1)}, u32[]{:S(2)}) copy-start(bf16[256,2048]{1,0:T(8,128)(2,1)} %param.11) | copy-start | bytes 3145732
  7.2 62.2 %all-gather.7.cloned.1.call-start = ((), (), s32[]{:S(2)}) async-start(), calls=%async_computation.2 | async-start | bytes 1114112 | tf_op jit(solution)/shard_map/all_gather | solution.py:106
  8.9 118.3 %all-gather.9.cloned.1.call-start = ((), (), s32[]{:S(2)}) async-start(), calls=%async_computation.3 | async-start | bytes 1114112 | tf_op jit(solution)/shard_map/all_gather | solution.py:107
  10.5 307.0 %reduce-scatter.3.cloned.1.call-start = ((), (), s32[]{:S(2)}) async-start(), calls=%async_computation.4 | async-start | bytes 2228224 | tf_op jit(solution)/shard_map/reduce_scatter | solution.py:149
  71.9 44.0 %copy-start.2 = (bf16[2,128,2048]{1,2,0:T(8,128)(2,1)}, bf16[2,128,2048]{1,2,0:T(8,128)(2,1)S(1)}, u32[]{:S(2)}) copy-start(bf16[2,128,2048]{1,2,0:T(8,128)(2,1)S(1)} %copy.25) | copy-start | bytes 3145732
  212.6 0.7 copy-start.4
  232.0 1.8 copy-start.1
  238.9 136.8 %copy-start.3 = (bf16[2,128,2048]{1,2,0:T(8,128)(2,1)S(1)}, bf16[2,128,2048]{1,2,0:T(8,128)(2,1)}, u32[]{:S(2)}) copy-start(bf16[2,128,2048]{1,2,0:T(8,128)(2,1)} %copy-done.2) | copy-start | bytes 3145732
  238.9 134.4 %all-gather.11.cloned.1.call-start = ((), (), s32[]{:S(2)}) async-start(), calls=%async_computation.5 | async-start | bytes 1114112 | tf_op jit(solution)/shard_map/all_gather | solution.py:153
  319.1 63.4 %reduce-scatter.5.cloned.1.call-start = ((), (), s32[]{:S(2)}) async-start(), calls=%async_computation.6 | async-start | bytes 196608 | tf_op jit(solution)/shard_map/reduce_scatter | solution.py:157
Sparse Core Ops, SparseCore 0:
  11.3 57.9 all-gather.6
  72.7 54.4 all-gather.8
  239.0 78.4 reduce-scatter.2
  320.7 52.6 all-gather.10
  376.0 6.4 reduce-scatter.4
where the time goes:
time: 391 us; the launch traced here: 389 us
  waiting for transfers between devices  196 us (50%)
  blocking collectives  117 us (30%)
  matrix products  21.1 us (5%)
  local copies, waits for them, and re-layouts  20 us (5%)
  other arithmetic  19.8 us (5%)
  between operations  13.9 us (4%)
    all_gather x3, blocking collectives, combined_all(): gathered = jax.tree.map(lambda a: lax.all_gather(a, axis), part)  117 us
    reduce_scatter x1, waiting for transfers between devices, per_device(): dq_home = lax.psum_scatter(dq_all, 'vis', scatter_dimension=1, tiled=True)  78.5 us
    all_gather x1, waiting for transfers between devices, per_device(): lax.all_gather(queries, 'vis', axis=1, tiled=True)  54.6 us
    all_gather x1, waiting for transfers between devices, per_device(): lax.all_gather(dq_low, 'vis', axis=1, tiled=True)  49.2 us
    add x15, other arithmetic, combine_stats(): total_new = first[1] * scale_first + second[1] * scale_second  11.3 us
    all_gather x1, waiting for transfers between devices, per_device(): lax.all_gather(d_out, 'vis', axis=1, tiled=True)  11.3 us
  transfers between devices with their start and end apart: 5, of which 5 were waited for; matrix products, arithmetic and copies ran while one was open for 5% of the time, Pallas kernels for 0%

commit v1 on v0

v1 whole, which is shorter than its diff:
```python
import functools
import math

import jax
import jax.numpy as jnp
from jax import lax
from jax.experimental import pallas as pl
from jax.experimental.pallas import tpu as pltpu
from jax.sharding import PartitionSpec as P

HQ = 32
KVH = 8
HD = 128
GROUPS = HQ // KVH
INV_ROOT = HD ** (-0.5)
NT = (((1,), (1,)), ((), ()))
TN = (((0,), (0,)), ((), ()))
NN = (((1,), (0,)), ((), ()))


def dot(x, y, dims):
    return lax.dot_general(x, y, dims, preferred_element_type=jnp.float32)


def kernel(
    outer, inner, heads,
    q_ref, g_ref, k_ref, v_ref, w_ref,
    din_ref, dk_ref, dv_ref,
    gath, probs, gprobs, stat, stat_in, stat_mid, stat_out, scal,
    dq_send, dq_plane, dq_mid, dq_line, gath2, part, part_send, part_in,
    gz_s, gz_r, gp_s, gp_r, sp_s, sp_r, sz_s, sz_r,
    rp_s, rp_r, rz_s, rz_r, hz_s, hz_r, hp_s, hp_r, hd_s, hd_r,
):
    batch, text, width = q_ref.shape
    kv_local = width // (HD * GROUPS)
    chunks = batch * kv_local
    vis = outer * inner
    rows = vis * GROUPS * text
    me = lax.axis_index("vis")
    my_head = lax.axis_index("head")
    line, place = me // inner, lax.rem(me, inner)

    def on_line(step):
        return lax.rem(line + step + outer, outer) * inner + place

    def in_plane(step):
        return line * inner + lax.rem(place + step + inner, inner)

    def other_head(step):
        return lax.rem(my_head + step + heads, heads)

    def copy(src, dst, send, recv, **where):
        return pltpu.make_async_remote_copy(
            src_ref=src, dst_ref=dst, send_sem=send, recv_sem=recv,
            device_id=where, device_id_type=pl.DeviceIdType.MESH,
        )

    barrier = pltpu.get_barrier_semaphore()
    for step in range(1, outer):
        pl.semaphore_signal(barrier, inc=1, device_id={"vis": on_line(step)},
                            device_id_type=pl.DeviceIdType.MESH)
    for step in range(1, inner):
        pl.semaphore_signal(barrier, inc=1, device_id={"vis": in_plane(step)},
                            device_id_type=pl.DeviceIdType.MESH)
    for step in range(1, heads):
        pl.semaphore_signal(barrier, inc=1, device_id={"head": other_head(step)},
                            device_id_type=pl.DeviceIdType.MESH)
    for which, ref in ((0, q_ref), (1, g_ref)):
        for b in range(batch):
            for h in range(kv_local):
                block = [
                    ref[b, :, pl.ds((h * GROUPS + g) * HD, HD)].astype(jnp.float32)
                    for g in range(GROUPS)
                ]
                gath[which, b * kv_local + h, me] = jnp.concatenate(block, 0).astype(jnp.bfloat16)
    pl.semaphore_wait(barrier, outer + inner + heads - 3)

    def gather(slot, line_s, line_r, plane_s, plane_r):
        sent = []

        def spread(step):
            owner = on_line(-step)
            for m in range(1, inner):
                c = copy(slot(owner), slot(owner), plane_s.at[step, m], plane_r.at[step, m],
                         vis=in_plane(m))
                c.start()
                sent.append(c)

        for step in range(1, outer):
            c = copy(slot(me), slot(me), line_s.at[step], line_r.at[step], vis=on_line(step))
            c.start()
            sent.append(c)
        spread(0)
        for step in range(1, outer):
            owner = on_line(-step)
            copy(slot(owner), slot(owner), line_s.at[step], line_r.at[step],
                 vis=on_line(step)).wait_recv()
            spread(step)
        for step in range(outer):
            for m in range(1, inner):
                owner = lax.rem(line - step + outer, outer) * inner + lax.rem(place - m + inner, inner)
                copy(slot(owner), slot(owner), plane_s.at[step, m], plane_r.at[step, m],
                     vis=in_plane(m)).wait_recv()
        return sent

    sent = gather(lambda v: gath.at[:, :, v], gz_s, gz_r, gp_s, gp_r)

    def first(c, _):
        b, h = c // kv_local, lax.rem(c, kv_local)
        lanes = pl.ds(pl.multiple_of(h * HD, HD), HD)
        query = gath[0, c].reshape(rows, HD)
        grad = gath[1, c].reshape(rows, HD)
        scores = dot(k_ref[b, :, lanes], query, NT) * INV_ROOT
        peak = jnp.max(scores, axis=0, keepdims=True)
        weights = jnp.exp(scores - peak)
        grads = dot(v_ref[b, :, lanes], grad, NT)
        probs[c] = weights
        gprobs[c] = grads
        stat[0, pl.ds(c, 1), :] = peak
        stat[1, pl.ds(c, 1), :] = jnp.sum(weights, axis=0, keepdims=True)
        stat[2, pl.ds(c, 1), :] = jnp.sum(weights * grads, axis=0, keepdims=True)
        return 0

    lax.fori_loop(0, chunks, first, 0)

    def combine(parts):
        peak = functools.reduce(jnp.maximum, [p[0] for p in parts])
        scale = [jnp.exp(p[0] - peak) for p in parts]
        total = sum(p[1] * s for p, s in zip(parts, scale))
        weighted = sum(p[2] * s for p, s in zip(parts, scale))
        return peak, total, weighted

    for m in range(1, inner):
        c = copy(stat, stat_in.at[m], sp_s.at[m], sp_r.at[m], vis=in_plane(m))
        c.start()
        sent.append(c)
    for m in range(1, inner):
        copy(stat, stat_in.at[m], sp_s.at[m], sp_r.at[m], vis=in_plane(m)).wait_recv()
    merged = combine([stat] + [stat_in.at[m] for m in range(1, inner)])
    for i in range(3):
        stat_mid[i] = merged[i]
    for step in range(1, outer):
        c = copy(stat_mid, stat_out.at[step], sz_s.at[step], sz_r.at[step], vis=on_line(step))
        c.start()
        sent.append(c)
    for step in range(1, outer):
        copy(stat_mid, stat_out.at[step], sz_s.at[step], sz_r.at[step],
             vis=on_line(step)).wait_recv()
    peak, total, weighted = combine([stat_mid] + [stat_out.at[s] for s in range(1, outer)])
    scal[0] = jnp.exp(stat[0] - peak) / total
    scal[1] = weighted / total

    def second(c, _):
        b, h = c // kv_local, lax.rem(c, kv_local)
        lanes = pl.ds(pl.multiple_of(h * HD, HD), HD)
        query = gath[0, c].reshape(rows, HD)
        grad = gath[1, c].reshape(rows, HD)
        prob = probs[c] * scal[0, pl.ds(c, 1), :]
        low = (prob * (gprobs[c] - scal[1, pl.ds(c, 1), :])).astype(jnp.bfloat16)
        dq = dot(low, k_ref[b, :, lanes], TN) * INV_ROOT
        dq_send[c] = dq.astype(jnp.bfloat16).reshape(outer, inner, GROUPS * text, HD)
        for m in range(1, inner):
            copy(dq_send.at[c, :, lax.rem(place + m, inner)], dq_plane.at[m, c],
                 rp_s.at[m, c], rp_r.at[m, c], vis=in_plane(m)).start()
        dk = dot(low, query, NN) * INV_ROOT
        dk_ref[b, :, lanes] = dk.astype(jnp.bfloat16)
        dv_ref[b, :, lanes] = dot(prob.astype(jnp.bfloat16), grad, NN).astype(jnp.bfloat16)
        return 0

    lax.fori_loop(0, chunks, second, 0)

    def arrived(c, _):
        for m in range(1, inner):
            d = copy(dq_send.at[c, :, lax.rem(place + m, inner)], dq_plane.at[m, c],
                     rp_s.at[m, c], rp_r.at[m, c], vis=in_plane(m))
            d.wait_send()
            d.wait_recv()
        return 0

    lax.fori_loop(0, chunks, arrived, 0)

    def plane_sum(owner_line):
        acc = dq_send[:, owner_line, place].astype(jnp.float32)
        for m in range(1, inner):
            acc += dq_plane[m, :, owner_line].astype(jnp.float32)
        return acc

    for step in range(1, outer):
        dq_mid[step] = plane_sum(lax.rem(line + step, outer)).astype(jnp.bfloat16)
        c = copy(dq_mid.at[step], dq_line.at[step], rz_s.at[step], rz_r.at[step], vis=on_line(step))
        c.start()
        sent.append(c)
    home = plane_sum(line)
    for step in range(1, outer):
        copy(dq_mid.at[step], dq_line.at[step], rz_s.at[step], rz_r.at[step],
             vis=on_line(step)).wait_recv()
        home += dq_line[step].astype(jnp.float32)
    for h in range(kv_local):
        for g in range(GROUPS):
            block = [home[b * kv_local + h, g * text:(g + 1) * text] for b in range(batch)]
            gath2[me, :, pl.ds((h * GROUPS + g) * HD, HD)] = jnp.concatenate(block, 0).astype(jnp.bfloat16)

    sent += gather(lambda v: gath2.at[v], hz_s, hz_r, hp_s, hp_r)

    cols = w_ref.shape[0]
    per_head = vis // heads
    product = dot(gath2[...].reshape(vis * batch * text, width), w_ref[...], NT)
    part[...] = product.reshape(heads, per_head * batch * text, cols)
    part_send[...] = product.astype(jnp.bfloat16).reshape(heads, per_head * batch * text, cols)
    for step in range(1, heads):
        c = copy(part_send.at[other_head(step)], part_in.at[step], hd_s.at[step], hd_r.at[step],
                 head=other_head(step))
        c.start()
        sent.append(c)
    mine = part[my_head]
    for step in range(1, heads):
        copy(part_send.at[other_head(step)], part_in.at[step], hd_s.at[step], hd_r.at[step],
             head=other_head(step)).wait_recv()
        mine += part_in[step].astype(jnp.float32)
    mine = mine.reshape(per_head, batch, text, cols)
    for b in range(batch):
        din_ref[b] = mine[:, b].reshape(per_head * text, cols).astype(jnp.bfloat16)
    for c in sent:
        c.wait_send()


def per_device(vis, heads, queries, keys, values, d_out, q_weight):
    batch, text, width = queries.shape
    kv_local = keys.shape[2] // HD
    chunks = batch * kv_local
    inner = math.gcd(vis, 4)
    outer = vis // inner
    block = GROUPS * text
    rows = vis * block
    tokens = keys.shape[1]
    cols = q_weight.shape[0]
    share = vis // heads * batch * text
    low, full = jnp.bfloat16, jnp.float32
    dma = pltpu.SemaphoreType.DMA
    scratch = [
        pltpu.VMEM((2, chunks, vis, block, HD), low),
        pltpu.VMEM((chunks, tokens, rows), full),
        pltpu.VMEM((chunks, tokens, rows), full),
        pltpu.VMEM((3, chunks, rows), full),
        pltpu.VMEM((inner, 3, chunks, rows), full),
        pltpu.VMEM((3, chunks, rows), full),
        pltpu.VMEM((outer, 3, chunks, rows), full),
        pltpu.VMEM((2, chunks, rows), full),
        pltpu.VMEM((chunks, outer, inner, block, HD), low),
        pltpu.VMEM((inner, chunks, outer, block, HD), low),
        pltpu.VMEM((outer, chunks, block, HD), low),
        pltpu.VMEM((outer, chunks, block, HD), low),
        pltpu.VMEM((vis, batch * text, width), low),
        pltpu.VMEM((heads, share, cols), full),
        pltpu.VMEM((heads, share, cols), low),
        pltpu.VMEM((heads, share, cols), low),
        dma((outer,)), dma((outer,)), dma((outer, inner)), dma((outer, inner)),
        dma((inner,)), dma((inner,)), dma((outer,)), dma((outer,)),
        dma((inner, chunks)), dma((inner, chunks)), dma((outer,)), dma((outer,)),
        dma((outer,)), dma((outer,)), dma((outer, inner)), dma((outer, inner)),
        dma((heads,)), dma((heads,)),
    ]
    return pl.pallas_call(
        functools.partial(kernel, outer, inner, heads),
        out_shape=(
            jax.ShapeDtypeStruct((batch, vis * text // heads, cols), low),
            jax.ShapeDtypeStruct(keys.shape, low),
            jax.ShapeDtypeStruct(values.shape, low),
        ),
        in_specs=[pl.BlockSpec(memory_space=pltpu.VMEM)] * 5,
        out_specs=(pl.BlockSpec(memory_space=pltpu.VMEM),) * 3,
        scratch_shapes=scratch,
        compiler_params=pltpu.CompilerParams(
            collective_id=0, has_side_effects=True, vmem_limit_bytes=50 * 1024 * 1024
        ),
    )(queries, d_out, keys, values, q_weight)


def solution(mesh):
    placed = (
        P(None, "vis", "head"),
        P(None, "vis", "head"),
        P(None, "vis", "head"),
        P(None, "vis", "head"),
        P("vis", "head"),
    )
    return jax.shard_map(
        functools.partial(per_device, mesh.shape["vis"], mesh.shape["head"]),
        mesh=mesh,
        in_specs=placed,
        out_specs=(P(None, "head", "vis"), P(None, "vis", "head"), P(None, "vis", "head")),
        check_vma=False,
    )
```

time: 391 us -> 84.2 us (0.22)
  waiting for transfers between devices: 196 us -> 0 us
  blocking collectives: 117 us -> 0 us
  Pallas kernels: 0 us -> 76.8 us
  matrix products: 21.1 us -> 0 us
  other arithmetic: 19.8 us -> 0 us
  local copies, waits for them, and re-layouts: 20 us -> 6.37 us
  between operations: 13.9 us -> 0.65 us
    all_gather x3 -> x0, blocking collectives: 117 us -> none  [combined_all(): gathered = jax.tree.map(lambda a: lax.all_gather(a, axis), part)]
    all_gather x3 -> x0, waiting for transfers between devices: 115 us -> none  [the longest x1 54.6 us: per_device(): lax.all_gather(queries, 'vis', axis=1, tiled=True)]
    reduce_scatter x2 -> x0, waiting for transfers between devices: 81.3 us -> none  [the longest x1 78.5 us: per_device(): dq_home = lax.psum_scatter(dq_all, 'vis', scatter_dimension=1, tiled=True)]
    pallas_call x0 -> x1, Pallas kernels: none -> 76.8 us  [per_device(): pl.pallas_call(functools.partial(kernel, outer, inner, heads), out_shape=...]
    dot_general x6 -> x0, matrix products: 21.1 us -> none  [the longest x1 5.83 us: grad_products(): jnp.einsum('brkgd,bjkd->bkgrj', split_query(grad_block), split_key(value_...]
    add x31 -> x0, other arithmetic: 11.8 us -> none  [the longest x15 11.3 us: combine_stats(): total_new = first[1] * scale_first + second[1] * scale_second]
    convert_element_type x2 -> x0, other arithmetic: 7.91 us -> none  [the longest x1 6.37 us: local_grads(): (probs * (grad_probs - delta_part[..., None])).astype(jnp.bfloat16)]
    reshape x3 -> x0, local copies, waits for them, and re-layouts: 7.14 us -> none  [the longest x2 4.26 us: split_key(): return block.reshape(block.shape[0], block.shape[1], -1, HD)]
  transfers between devices with their start and end apart: 5 -> 0, of which waited for: 5 -> 0; matrix products, arithmetic and copies ran while one was open for 5% -> 0% of each run, Pallas kernels for 0% -> 0%
where the time goes in v1:
time: 84.2 us; the launch traced here: 83.9 us
  Pallas kernels  76.8 us (91%)
  local copies, waits for them, and re-layouts  6.37 us (8%)
    pallas_call x1, Pallas kernels, per_device(): pl.pallas_call(functools.partial(kernel, outer, inner, heads), out_shape=...  76.8 us
    unnamed x11, local copies, waits for them, and re-layouts  6.37 us

profile of v1, /device:TPU:0, one launch (start us, length us, event | category | flops | bytes accessed | tf_op | source)
XLA Modules:
  0.0 83.9 jit_solution(2685440704553181567)
XLA Ops:
  0.6 0.0 copy-start
  0.6 1.1 %copy-done = bf16[2,400,512]{2,1,0:T(8,128)(2,1)S(1)} copy-done((bf16[2,400,512]{2,1,0:T(8,128)(2,1)S(1)}, bf16[2,400,512]{2,1,0:T(8,128)(2,1)}, u32[]{:S(2)}) %copy-start) | copy-done | bytes 819224
  1.8 0.0 copy-start.1
  1.8 1.1 %copy-done.1 = bf16[2,400,512]{2,1,0:T(8,128)(2,1)S(1)} copy-done((bf16[2,400,512]{2,1,0:T(8,128)(2,1)S(1)}, bf16[2,400,512]{2,1,0:T(8,128)(2,1)}, u32[]{:S(2)}) %copy-start.1) | copy-done | bytes 819224
  2.9 0.0 copy-start.2
  2.9 0.8 copy-done.2
  3.8 0.0 copy-start.3
  3.8 0.8 copy-done.3
  4.6 76.8 %shard_map.76 = (bf16[2,64,256]{2,1,0:T(8,128)(2,1)S(1)}, bf16[2,400,512]{2,1,0:T(8,128)(2,1)S(1)}, bf16[2,400,512]{2,1,0:T(8,128)(2,1)S(1)}) custom-call(bf16[2,8,2048]{2,1,0:T(8,128)(2,1)S(1)} %copy-done.2, bf16[2,8,2048]{2,1,0:T(8,128)(2,1)S(1)} %copy-done.3, bf16[2,400,512]{2,1,0:T(8,128)(2,1)S(1)} %copy-done, bf16[2,400,512]{2,1,0:T(8,128)(2,1)S(1)} %copy-done.1, ...), custom_call_target="tpu_custom_call" | custom-call | tf_op jit(solution)/shard_map/pallas_call | solution.py:263
  81.5 0.6 copy.11
  82.1 0.9 %copy.12 = bf16[2,400,512]{2,1,0:T(8,128)(2,1)} copy(bf16[2,400,512]{2,1,0:T(8,128)(2,1)S(1)} %get-tuple-element.7) | data formatting | bytes 1638400
  83.0 0.9 %copy.13 = bf16[2,400,512]{2,1,0:T(8,128)(2,1)} copy(bf16[2,400,512]{2,1,0:T(8,128)(2,1)S(1)} %get-tuple-element.8) | data formatting | bytes 1638400
Async XLA Ops:
  0.6 1.1 %copy-start = (bf16[2,400,512]{2,1,0:T(8,128)(2,1)S(1)}, bf16[2,400,512]{2,1,0:T(8,128)(2,1)}, u32[]{:S(2)}) copy-start(bf16[2,400,512]{2,1,0:T(8,128)(2,1)} %k_ref.1) | copy-start | bytes 2457604
  1.8 1.1 %copy-start.1 = (bf16[2,400,512]{2,1,0:T(8,128)(2,1)S(1)}, bf16[2,400,512]{2,1,0:T(8,128)(2,1)}, u32[]{:S(2)}) copy-start(bf16[2,400,512]{2,1,0:T(8,128)(2,1)} %v_ref.1) | copy-start | bytes 2457604
  2.9 0.8 %copy-start.2 = (bf16[2,8,2048]{2,1,0:T(8,128)(2,1)S(1)}, bf16[2,8,2048]{2,1,0:T(8,128)(2,1)}, u32[]{:S(2)}) copy-start(bf16[2,8,2048]{2,1,0:T(8,128)(2,1)} %q_ref.1) | copy-start | bytes 196612
  3.8 0.8 %copy-start.3 = (bf16[2,8,2048]{2,1,0:T(8,128)(2,1)S(1)}, bf16[2,8,2048]{2,1,0:T(8,128)(2,1)}, u32[]{:S(2)}) copy-start(bf16[2,8,2048]{2,1,0:T(8,128)(2,1)} %g_ref.1) | copy-start | bytes 196612

commit v2 on v1

--- a/solution.py
+++ b/solution.py
@@ -24,8 +24,9 @@
 
 def kernel(
     outer, inner, heads,
-    q_ref, g_ref, k_ref, v_ref, w_ref,
+    q_hbm, g_hbm, k_hbm, v_hbm, w_hbm,
     din_ref, dk_ref, dv_ref,
+    q_ref, g_ref, k_ref, v_ref, w_ref, load,
     gath, probs, gprobs, stat, stat_in, stat_mid, stat_out, scal,
     dq_send, dq_plane, dq_mid, dq_line, gath2, part, part_send, part_in,
     gz_s, gz_r, gp_s, gp_r, sp_s, sp_r, sz_s, sz_r,
@@ -55,6 +56,14 @@
             device_id=where, device_id_type=pl.DeviceIdType.MESH,
         )
 
+    loads = [
+        pltpu.make_async_copy(src, dst, load.at[i])
+        for i, (src, dst) in enumerate((
+            (q_hbm, q_ref), (g_hbm, g_ref), (k_hbm, k_ref), (v_hbm, v_ref), (w_hbm, w_ref)
+        ))
+    ]
+    for d in loads:
+        d.start()
     barrier = pltpu.get_barrier_semaphore()
     for step in range(1, outer):
         pl.semaphore_signal(barrier, inc=1, device_id={"vis": on_line(step)},
@@ -65,6 +74,8 @@
     for step in range(1, heads):
         pl.semaphore_signal(barrier, inc=1, device_id={"head": other_head(step)},
                             device_id_type=pl.DeviceIdType.MESH)
+    loads[0].wait()
+    loads[1].wait()
     for which, ref in ((0, q_ref), (1, g_ref)):
         for b in range(batch):
             for h in range(kv_local):
@@ -105,6 +116,9 @@
 
     sent = gather(lambda v: gath.at[:, :, v], gz_s, gz_r, gp_s, gp_r)
 
+    loads[2].wait()
+    loads[3].wait()
+
     def first(c, _):
         b, h = c // kv_local, lax.rem(c, kv_local)
         lanes = pl.ds(pl.multiple_of(h * HD, HD), HD)
@@ -202,6 +216,7 @@
 
     sent += gather(lambda v: gath2.at[v], hz_s, hz_r, hp_s, hp_r)
 
+    loads[4].wait()
     cols = w_ref.shape[0]
     per_head = vis // heads
     product = dot(gath2[...].reshape(vis * batch * text, width), w_ref[...], NT)
@@ -238,6 +253,12 @@
     low, full = jnp.bfloat16, jnp.float32
     dma = pltpu.SemaphoreType.DMA
     scratch = [
+        pltpu.VMEM(queries.shape, low),
+        pltpu.VMEM(d_out.shape, low),
+        pltpu.VMEM(keys.shape, low),
+        pltpu.VMEM(values.shape, low),
+        pltpu.VMEM(q_weight.shape, low),
+        dma((5,)),
         pltpu.VMEM((2, chunks, vis, block, HD), low),
         pltpu.VMEM((chunks, tokens, rows), full),
         pltpu.VMEM((chunks, tokens, rows), full),
@@ -267,7 +288,7 @@
             jax.ShapeDtypeStruct(keys.shape, low),
             jax.ShapeDtypeStruct(values.shape, low),
         ),
-        in_specs=[pl.BlockSpec(memory_space=pltpu.VMEM)] * 5,
+        in_specs=[pl.BlockSpec(memory_space=pltpu.HBM)] * 5,
         out_specs=(pl.BlockSpec(memory_space=pltpu.VMEM),) * 3,
         scratch_shapes=scratch,
         compiler_params=pltpu.CompilerParams(

time: 84.2 us -> 83.3 us (0.989)
  no operation moved by 1% of the time
where the time goes in v2:
time: 83.3 us; the launch traced here: 83 us
  Pallas kernels  76 us (91%)
  local copies, waits for them, and re-layouts  6.37 us (8%)
    pallas_call x1, Pallas kernels, per_device(): pl.pallas_call(functools.partial(kernel, outer, inner, heads), out_shape=...  76 us
    unnamed x11, local copies, waits for them, and re-layouts  6.37 us

profile of v2, /device:TPU:0, one launch (start us, length us, event | category | flops | bytes accessed | tf_op | source)
XLA Modules:
  0.0 83.0 jit_solution(5636651001814795768)
XLA Ops:
  0.6 0.0 copy-start
  0.6 1.1 %copy-done = bf16[2,400,512]{2,1,0:T(8,128)(2,1)S(1)} copy-done((bf16[2,400,512]{2,1,0:T(8,128)(2,1)S(1)}, bf16[2,400,512]{2,1,0:T(8,128)(2,1)}, u32[]{:S(2)}) %copy-start) | copy-done | bytes 819224
  1.8 0.0 copy-start.1
  1.8 1.1 %copy-done.1 = bf16[2,400,512]{2,1,0:T(8,128)(2,1)S(1)} copy-done((bf16[2,400,512]{2,1,0:T(8,128)(2,1)S(1)}, bf16[2,400,512]{2,1,0:T(8,128)(2,1)}, u32[]{:S(2)}) %copy-start.1) | copy-done | bytes 819224
  2.9 0.0 copy-start.2
  2.9 0.8 %copy-done.2 = bf16[2,8,2048]{2,1,0:T(8,128)(2,1)S(1)} copy-done((bf16[2,8,2048]{2,1,0:T(8,128)(2,1)S(1)}, bf16[2,8,2048]{2,1,0:T(8,128)(2,1)}, u32[]{:S(2)}) %copy-start.2) | copy-done | bytes 65560
  3.8 0.0 copy-start.3
  3.8 0.8 %copy-done.3 = bf16[2,8,2048]{2,1,0:T(8,128)(2,1)S(1)} copy-done((bf16[2,8,2048]{2,1,0:T(8,128)(2,1)S(1)}, bf16[2,8,2048]{2,1,0:T(8,128)(2,1)}, u32[]{:S(2)}) %copy-start.3) | copy-done | bytes 65560
  4.6 76.0 %shard_map.76 = (bf16[2,64,256]{2,1,0:T(8,128)(2,1)S(1)}, bf16[2,400,512]{2,1,0:T(8,128)(2,1)S(1)}, bf16[2,400,512]{2,1,0:T(8,128)(2,1)S(1)}) custom-call(bf16[2,8,2048]{2,1,0:T(8,128)(2,1)S(1)} %copy-done.2, bf16[2,8,2048]{2,1,0:T(8,128)(2,1)S(1)} %copy-done.3, bf16[2,400,512]{2,1,0:T(8,128)(2,1)S(1)} %copy-done, bf16[2,400,512]{2,1,0:T(8,128)(2,1)S(1)} %copy-done.1, ...), custom_call_target="tpu_custom_call" | custom-call | tf_op jit(solution)/shard_map/pallas_call | solution.py:284
  80.6 0.6 copy.11
  81.3 0.9 %copy.12 = bf16[2,400,512]{2,1,0:T(8,128)(2,1)} copy(bf16[2,400,512]{2,1,0:T(8,128)(2,1)S(1)} %get-tuple-element.7) | data formatting | bytes 1638400
  82.1 0.9 %copy.13 = bf16[2,400,512]{2,1,0:T(8,128)(2,1)} copy(bf16[2,400,512]{2,1,0:T(8,128)(2,1)S(1)} %get-tuple-element.8) | data formatting | bytes 1638400
Async XLA Ops:
  0.6 1.1 %copy-start = (bf16[2,400,512]{2,1,0:T(8,128)(2,1)S(1)}, bf16[2,400,512]{2,1,0:T(8,128)(2,1)}, u32[]{:S(2)}) copy-start(bf16[2,400,512]{2,1,0:T(8,128)(2,1)} %k_hbm.1) | copy-start | bytes 2457604
  1.8 1.1 %copy-start.1 = (bf16[2,400,512]{2,1,0:T(8,128)(2,1)S(1)}, bf16[2,400,512]{2,1,0:T(8,128)(2,1)}, u32[]{:S(2)}) copy-start(bf16[2,400,512]{2,1,0:T(8,128)(2,1)} %v_hbm.1) | copy-start | bytes 2457604
  2.9 0.8 %copy-start.2 = (bf16[2,8,2048]{2,1,0:T(8,128)(2,1)S(1)}, bf16[2,8,2048]{2,1,0:T(8,128)(2,1)}, u32[]{:S(2)}) copy-start(bf16[2,8,2048]{2,1,0:T(8,128)(2,1)} %q_hbm.1) | copy-start | bytes 196612
  3.8 0.8 %copy-start.3 = (bf16[2,8,2048]{2,1,0:T(8,128)(2,1)S(1)}, bf16[2,8,2048]{2,1,0:T(8,128)(2,1)}, u32[]{:S(2)}) copy-start(bf16[2,8,2048]{2,1,0:T(8,128)(2,1)} %g_hbm.1) | copy-start | bytes 196612

commit v3 on v2

--- a/solution.py
+++ b/solution.py
@@ -25,11 +25,12 @@
 def kernel(
     outer, inner, heads,
     q_hbm, g_hbm, k_hbm, v_hbm, w_hbm,
-    din_ref, dk_ref, dv_ref,
+    din_ref, dk_hbm, dv_hbm,
+    dk_ref, dv_ref, store,
     q_ref, g_ref, k_ref, v_ref, w_ref, load,
-    gath, probs, gprobs, stat, stat_in, stat_mid, stat_out, scal,
+    gath, probs, gprobs, stat, stat_in, stat_mid, stat_out, final, scal,
     dq_send, dq_plane, dq_mid, dq_line, gath2, part, part_send, part_in,
-    gz_s, gz_r, gp_s, gp_r, sp_s, sp_r, sz_s, sz_r,
+    gz_s, gz_r, gp_s, gp_r, sp_s, sp_r, sz_s, sz_r, sf_s, sf_r,
     rp_s, rp_r, rz_s, rz_r, hz_s, hz_r, hp_s, hp_r, hd_s, hd_r,
 ):
     batch, text, width = q_ref.shape
@@ -86,35 +87,59 @@
                 gath[which, b * kv_local + h, me] = jnp.concatenate(block, 0).astype(jnp.bfloat16)
     pl.semaphore_wait(barrier, outer + inner + heads - 3)
 
+    def flip(bit):
+        return line * inner + place + bit * (1 - 2 * lax.rem(place // bit, 2))
+
     def gather(slot, line_s, line_r, plane_s, plane_r):
         sent = []
 
-        def spread(step):
-            owner = on_line(-step)
-            for m in range(1, inner):
-                c = copy(slot(owner), slot(owner), plane_s.at[step, m], plane_r.at[step, m],
-                         vis=in_plane(m))
-                c.start()
-                sent.append(c)
-
-        for step in range(1, outer):
-            c = copy(slot(me), slot(me), line_s.at[step], line_r.at[step], vis=on_line(step))
+        def owner_of(step, bits):
+            column = place
+            for bit in bits:
+                column = column + bit * (1 - 2 * lax.rem(place // bit, 2))
+            return lax.rem(line - step + outer, outer) * inner + column
+
+        def plane_copy(step, i, owner, half, bit):
+            return copy(slot(owner, half), slot(owner, half), plane_s.at[step, i],
+                        plane_r.at[step, i], vis=flip(bit))
+
+        def begin(c):
             c.start()
             sent.append(c)
+
+        def line_copy(step, owner, half):
+            return copy(slot(owner, half), slot(owner, half), line_s.at[step, half],
+                        line_r.at[step, half], vis=on_line(step))
+
+        def spread(step):
+            owner = owner_of(step, ())
+            for half, bit in ((0, 1), (1, 2), (1, 1), (0, 2)):
+                begin(plane_copy(step, half + 2 * (bit - 1), owner, half, bit))
+
+        def relay(step):
+            plane_copy(step, 0, owner_of(step, (1,)), 0, 1).wait_recv()
+            begin(plane_copy(step, 4, owner_of(step, (1,)), 0, 2))
+            plane_copy(step, 3, owner_of(step, (2,)), 1, 2).wait_recv()
+            begin(plane_copy(step, 5, owner_of(step, (2,)), 1, 1))
+
+        for step in range(1, outer):
+            for half in range(2):
+                begin(line_copy(step, me, half))
         spread(0)
         for step in range(1, outer):
-            owner = on_line(-step)
-            copy(slot(owner), slot(owner), line_s.at[step], line_r.at[step],
-                 vis=on_line(step)).wait_recv()
+            for half in range(2):
+                line_copy(step, owner_of(step, ()), half).wait_recv()
             spread(step)
+            relay(step - 1)
+        relay(outer - 1)
         for step in range(outer):
-            for m in range(1, inner):
-                owner = lax.rem(line - step + outer, outer) * inner + lax.rem(place - m + inner, inner)
-                copy(slot(owner), slot(owner), plane_s.at[step, m], plane_r.at[step, m],
-                     vis=in_plane(m)).wait_recv()
+            plane_copy(step, 1, owner_of(step, (1,)), 1, 1).wait_recv()
+            plane_copy(step, 2, owner_of(step, (2,)), 0, 2).wait_recv()
+            plane_copy(step, 4, owner_of(step, (1, 2)), 0, 2).wait_recv()
+            plane_copy(step, 5, owner_of(step, (1, 2)), 1, 1).wait_recv()
         return sent
 
-    sent = gather(lambda v: gath.at[:, :, v], gz_s, gz_r, gp_s, gp_r)
+    sent = gather(lambda v, half: gath.at[half, :, v], gz_s, gz_r, gp_s, gp_r)
 
     loads[2].wait()
     loads[3].wait()
@@ -144,25 +169,47 @@
         weighted = sum(p[2] * s for p, s in zip(parts, scale))
         return peak, total, weighted
 
+    span = rows // inner
+
+    def lanes_of(step):
+        return pl.ds(pl.multiple_of(lax.rem(place + step + inner, inner) * span, span), span)
+
+    def plane_stat(m):
+        return copy(stat.at[:, :, lanes_of(m)], stat_in.at[m], sp_s.at[m], sp_r.at[m], vis=in_plane(m))
+
+    def line_stat(step):
+        return copy(stat_mid, stat_out.at[step], sz_s.at[step], sz_r.at[step], vis=on_line(step))
+
+    def final_stat(m, lanes):
+        return copy(final.at[:, :, lanes], final.at[:, :, lanes], sf_s.at[m], sf_r.at[m], vis=in_plane(m))
+
     for m in range(1, inner):
-        c = copy(stat, stat_in.at[m], sp_s.at[m], sp_r.at[m], vis=in_plane(m))
-        c.start()
-        sent.append(c)
+        c = plane_stat(m)
+        c.start()
+        sent.append(c)
+    stat_in[0] = stat[:, :, lanes_of(0)]
     for m in range(1, inner):
-        copy(stat, stat_in.at[m], sp_s.at[m], sp_r.at[m], vis=in_plane(m)).wait_recv()
-    merged = combine([stat] + [stat_in.at[m] for m in range(1, inner)])
+        plane_stat(m).wait_recv()
+    merged = combine([stat_in.at[m] for m in range(inner)])
     for i in range(3):
         stat_mid[i] = merged[i]
     for step in range(1, outer):
-        c = copy(stat_mid, stat_out.at[step], sz_s.at[step], sz_r.at[step], vis=on_line(step))
-        c.start()
-        sent.append(c)
-    for step in range(1, outer):
-        copy(stat_mid, stat_out.at[step], sz_s.at[step], sz_r.at[step],
-             vis=on_line(step)).wait_recv()
+        c = line_stat(step)
+        c.start()
+        sent.append(c)
+    for step in range(1, outer):
+        line_stat(step).wait_recv()
     peak, total, weighted = combine([stat_mid] + [stat_out.at[s] for s in range(1, outer)])
-    scal[0] = jnp.exp(stat[0] - peak) / total
-    scal[1] = weighted / total
+    final[0, :, lanes_of(0)] = peak + jnp.log(total)
+    final[1, :, lanes_of(0)] = weighted / total
+    for m in range(1, inner):
+        c = final_stat(m, lanes_of(0))
+        c.start()
+        sent.append(c)
+    for m in range(1, inner):
+        final_stat(m, lanes_of(-m)).wait_recv()
+    scal[0] = jnp.exp(stat[0] - final[0])
+    scal[1] = final[1]
 
     def second(c, _):
         b, h = c // kv_local, lax.rem(c, kv_local)
@@ -183,6 +230,13 @@
 
     lax.fori_loop(0, chunks, second, 0)
 
+    saves = [
+        pltpu.make_async_copy(dk_ref, dk_hbm, store.at[0]),
+        pltpu.make_async_copy(dv_ref, dv_hbm, store.at[1]),
+    ]
+    for d in saves:
+        d.start()
+
     def arrived(c, _):
         for m in range(1, inner):
             d = copy(dq_send.at[c, :, lax.rem(place + m, inner)], dq_plane.at[m, c],
@@ -214,7 +268,7 @@
             block = [home[b * kv_local + h, g * text:(g + 1) * text] for b in range(batch)]
             gath2[me, :, pl.ds((h * GROUPS + g) * HD, HD)] = jnp.concatenate(block, 0).astype(jnp.bfloat16)
 
-    sent += gather(lambda v: gath2.at[v], hz_s, hz_r, hp_s, hp_r)
+    sent += gather(lambda v, half: gath2.at[v, :, pl.ds(half * (width // 2), width // 2)], hz_s, hz_r, hp_s, hp_r)
 
     loads[4].wait()
     cols = w_ref.shape[0]
@@ -237,6 +291,17 @@
         din_ref[b] = mine[:, b].reshape(per_head * text, cols).astype(jnp.bfloat16)
     for c in sent:
         c.wait_send()
+    for d in saves:
+        d.wait()
+
+
+def leave(*refs):
+    count = len(refs) // 2
+    moves = [pltpu.make_async_copy(refs[i], refs[count + i], refs[-1].at[i]) for i in range(count)]
+    for d in moves:
+        d.start()
+    for d in moves:
+        d.wait()
 
 
 def per_device(vis, heads, queries, keys, values, d_out, q_weight):
@@ -253,6 +318,9 @@
     low, full = jnp.bfloat16, jnp.float32
     dma = pltpu.SemaphoreType.DMA
     scratch = [
+        pltpu.VMEM(keys.shape, low),
+        pltpu.VMEM(values.shape, low),
+        dma((2,)),
         pltpu.VMEM(queries.shape, low),
         pltpu.VMEM(d_out.shape, low),
         pltpu.VMEM(keys.shape, low),
@@ -263,9 +331,10 @@
         pltpu.VMEM((chunks, tokens, rows), full),
         pltpu.VMEM((chunks, tokens, rows), full),
         pltpu.VMEM((3, chunks, rows), full),
-        pltpu.VMEM((inner, 3, chunks, rows), full),
-        pltpu.VMEM((3, chunks, rows), full),
-        pltpu.VMEM((outer, 3, chunks, rows), full),
+        pltpu.VMEM((inner, 3, chunks, rows // inner), full),
+        pltpu.VMEM((3, chunks, rows // inner), full),
+        pltpu.VMEM((outer, 3, chunks, rows // inner), full),
+        pltpu.VMEM((2, chunks, rows), full),
         pltpu.VMEM((2, chunks, rows), full),
         pltpu.VMEM((chunks, outer, inner, block, HD), low),
         pltpu.VMEM((inner, chunks, outer, block, HD), low),
@@ -275,13 +344,13 @@
         pltpu.VMEM((heads, share, cols), full),
         pltpu.VMEM((heads, share, cols), low),
         pltpu.VMEM((heads, share, cols), low),
-        dma((outer,)), dma((outer,)), dma((outer, inner)), dma((outer, inner)),
-        dma((inner,)), dma((inner,)), dma((outer,)), dma((outer,)),
+        dma((outer, 2)), dma((outer, 2)), dma((outer, 6)), dma((outer, 6)),
+        dma((inner,)), dma((inner,)), dma((outer,)), dma((outer,)), dma((inner,)), dma((inner,)),
         dma((inner, chunks)), dma((inner, chunks)), dma((outer,)), dma((outer,)),
-        dma((outer,)), dma((outer,)), dma((outer, inner)), dma((outer, inner)),
+        dma((outer, 2)), dma((outer, 2)), dma((outer, 6)), dma((outer, 6)),
         dma((heads,)), dma((heads,)),
     ]
-    return pl.pallas_call(
+    results = pl.pallas_call(
         functools.partial(kernel, outer, inner, heads),
         out_shape=(
             jax.ShapeDtypeStruct((batch, vis * text // heads, cols), low),
@@ -289,12 +358,19 @@
             jax.ShapeDtypeStruct(values.shape, low),
         ),
         in_specs=[pl.BlockSpec(memory_space=pltpu.HBM)] * 5,
-        out_specs=(pl.BlockSpec(memory_space=pltpu.VMEM),) * 3,
+        out_specs=(pl.BlockSpec(memory_space=pltpu.VMEM),) + (pl.BlockSpec(memory_space=pltpu.HBM),) * 2,
         scratch_shapes=scratch,
         compiler_params=pltpu.CompilerParams(
-            collective_id=0, has_side_effects=True, vmem_limit_bytes=50 * 1024 * 1024
+            collective_id=0, has_side_effects=True, vmem_limit_bytes=60 * 1024 * 1024
         ),
     )(queries, d_out, keys, values, q_weight)
+    return pl.pallas_call(
+        leave,
+        out_shape=tuple(jax.ShapeDtypeStruct(x.shape, x.dtype) for x in results),
+        in_specs=[pl.BlockSpec(memory_space=pltpu.VMEM)] * len(results),
+        out_specs=(pl.BlockSpec(memory_space=pltpu.HBM),) * len(results),
+        scratch_shapes=[dma((len(results),))],
+    )(*results)
 
 
 def solution(mesh):

time: 83.3 us -> 80.2 us (0.963)
  local copies, waits for them, and re-layouts: 6.37 us -> 0 us
  Pallas kernels: 76 us -> 79.4 us
    unnamed x11 -> x0, local copies, waits for them, and re-layouts: 6.37 us -> none
    pallas_call x0 -> x1, Pallas kernels: none -> 2.62 us  [per_device(): pl.pallas_call(leave, out_shape=tuple((jax.ShapeDtypeStruct(x.shape, x.dt...]
where the time goes in v3:
time: 80.2 us; the launch traced here: 80 us
  Pallas kernels  79.4 us (99%)
    pallas_call x1, Pallas kernels, per_device(): pl.pallas_call(functools.partial(kernel, outer, inner, heads), out_shape=...  76.8 us
    pallas_call x1, Pallas kernels, per_device(): pl.pallas_call(leave, out_shape=tuple((jax.ShapeDtypeStruct(x.shape, x.dt...  2.62 us

profile of v3, /device:TPU:0, one launch (start us, length us, event | category | flops | bytes accessed | tf_op | source)
XLA Modules:
  0.0 80.0 jit_solution(5247262481481399830)
XLA Ops:
  0.6 76.8 %shard_map.76 = (bf16[2,64,256]{2,1,0:T(8,128)(2,1)}, bf16[2,400,512]{2,1,0:T(8,128)(2,1)}, bf16[2,400,512]{2,1,0:T(8,128)(2,1)}) custom-call(bf16[2,8,2048]{2,1,0:T(8,128)(2,1)} %q_hbm.1, bf16[2,8,2048]{2,1,0:T(8,128)(2,1)} %g_hbm.1, bf16[2,400,512]{2,1,0:T(8,128)(2,1)} %k_hbm.1, bf16[2,400,512]{2,1,0:T(8,128)(2,1)} %v_hbm.1, bf16[256,2048]{1,0:T(8,128)(2,1)} %w_hbm.1), custom_call_target="tpu_custom_call" | custom-call | tf_op jit(solution)/shard_map/pallas_call | solution.py:353
  77.4 2.6 %shard_map.77 = (bf16[2,64,256]{2,1,0:T(8,128)(2,1)}, bf16[2,400,512]{2,1,0:T(8,128)(2,1)}, bf16[2,400,512]{2,1,0:T(8,128)(2,1)}) custom-call(bf16[2,64,256]{2,1,0:T(8,128)(2,1)} %get-tuple-element.6.refs_0_, bf16[2,400,512]{2,1,0:T(8,128)(2,1)} %get-tuple-element.7.refs_1_, bf16[2,400,512]{2,1,0:T(8,128)(2,1)} %get-tuple-element.8.refs_2_), custom_call_target="tpu_custom_call" | custom-call | tf_op jit(solution)/shard_map/pallas_call | solution.py:367

commit v4 on v3

--- a/solution.py
+++ b/solution.py
@@ -126,20 +126,37 @@
             for half in range(2):
                 begin(line_copy(step, me, half))
         spread(0)
-        for step in range(1, outer):
-            for half in range(2):
-                line_copy(step, owner_of(step, ()), half).wait_recv()
-            spread(step)
-            relay(step - 1)
-        relay(outer - 1)
-        for step in range(outer):
+
+        def forward():
+            for step in range(1, outer):
+                for half in range(2):
+                    line_copy(step, owner_of(step, ()), half).wait_recv()
+                spread(step)
+                relay(step - 1)
+            relay(outer - 1)
+
+        def finish():
+            for step in range(outer):
+                finish_step(step)
+
+        def finish_step(step):
             plane_copy(step, 1, owner_of(step, (1,)), 1, 1).wait_recv()
             plane_copy(step, 2, owner_of(step, (2,)), 0, 2).wait_recv()
             plane_copy(step, 4, owner_of(step, (1, 2)), 0, 2).wait_recv()
             plane_copy(step, 5, owner_of(step, (1, 2)), 1, 1).wait_recv()
-        return sent
-
-    sent = gather(lambda v, half: gath.at[half, :, v], gz_s, gz_r, gp_s, gp_r)
+        return sent, forward, finish
+
+    sent = []
+    gathers = []
+    for b in range(batch):
+        mine = pl.ds(b * kv_local, kv_local)
+        gathers.append(gather(
+            lambda v, half, mine=mine: gath.at[half, mine, v],
+            gz_s.at[b], gz_r.at[b], gp_s.at[b], gp_r.at[b],
+        ))
+    for more, forward, finish in gathers:
+        forward()
+        sent += more
 
     loads[2].wait()
     loads[3].wait()
@@ -160,7 +177,9 @@
         stat[2, pl.ds(c, 1), :] = jnp.sum(weights * grads, axis=0, keepdims=True)
         return 0
 
-    lax.fori_loop(0, chunks, first, 0)
+    for b in range(batch):
+        gathers[b][2]()
+        lax.fori_loop(b * kv_local, (b + 1) * kv_local, first, 0)
 
     def combine(parts):
         peak = functools.reduce(jnp.maximum, [p[0] for p in parts])
@@ -268,7 +287,10 @@
             block = [home[b * kv_local + h, g * text:(g + 1) * text] for b in range(batch)]
             gath2[me, :, pl.ds((h * GROUPS + g) * HD, HD)] = jnp.concatenate(block, 0).astype(jnp.bfloat16)
 
-    sent += gather(lambda v, half: gath2.at[v, :, pl.ds(half * (width // 2), width // 2)], hz_s, hz_r, hp_s, hp_r)
+    more, forward, finish = gather(lambda v, half: gath2.at[v, :, pl.ds(half * (width // 2), width // 2)], hz_s, hz_r, hp_s, hp_r)
+    forward()
+    sent += more
+    finish()
 
     loads[4].wait()
     cols = w_ref.shape[0]
@@ -344,7 +366,7 @@
         pltpu.VMEM((heads, share, cols), full),
         pltpu.VMEM((heads, share, cols), low),
         pltpu.VMEM((heads, share, cols), low),
-        dma((outer, 2)), dma((outer, 2)), dma((outer, 6)), dma((outer, 6)),
+        dma((batch, outer, 2)), dma((batch, outer, 2)), dma((batch, outer, 6)), dma((batch, outer, 6)),
         dma((inner,)), dma((inner,)), dma((outer,)), dma((outer,)), dma((inner,)), dma((inner,)),
         dma((inner, chunks)), dma((inner, chunks)), dma((outer,)), dma((outer,)),
         dma((outer, 2)), dma((outer, 2)), dma((outer, 6)), dma((outer, 6)),

time: 80.2 us -> 83 us (1.035)
  Pallas kernels: 79.4 us -> 82.2 us
    pallas_call x1, Pallas kernels: 76.8 us -> 79.5 us  [per_device(): pl.pallas_call(functools.partial(kernel, outer, inner, heads), out_shape=...]
where the time goes in v4:
time: 83 us; the launch traced here: 82.8 us
  Pallas kernels  82.2 us (99%)
    pallas_call x1, Pallas kernels, per_device(): pl.pallas_call(functools.partial(kernel, outer, inner, heads), out_shape=...  79.5 us
    pallas_call x1, Pallas kernels, per_device(): pl.pallas_call(leave, out_shape=tuple((jax.ShapeDtypeStruct(x.shape, x.dt...  2.62 us

profile of v4, /device:TPU:0, one launch (start us, length us, event | category | flops | bytes accessed | tf_op | source)
XLA Modules:
  0.0 82.8 jit_solution(1211744270057904164)
XLA Ops:
  0.6 79.5 %shard_map.76 = (bf16[2,64,256]{2,1,0:T(8,128)(2,1)}, bf16[2,400,512]{2,1,0:T(8,128)(2,1)}, bf16[2,400,512]{2,1,0:T(8,128)(2,1)}) custom-call(bf16[2,8,2048]{2,1,0:T(8,128)(2,1)} %q_hbm.1, bf16[2,8,2048]{2,1,0:T(8,128)(2,1)} %g_hbm.1, bf16[2,400,512]{2,1,0:T(8,128)(2,1)} %k_hbm.1, bf16[2,400,512]{2,1,0:T(8,128)(2,1)} %v_hbm.1, bf16[256,2048]{1,0:T(8,128)(2,1)} %w_hbm.1), custom_call_target="tpu_custom_call" | custom-call | tf_op jit(solution)/shard_map/pallas_call | solution.py:375
  80.2 2.6 %shard_map.77 = (bf16[2,64,256]{2,1,0:T(8,128)(2,1)}, bf16[2,400,512]{2,1,0:T(8,128)(2,1)}, bf16[2,400,512]{2,1,0:T(8,128)(2,1)}) custom-call(bf16[2,64,256]{2,1,0:T(8,128)(2,1)} %get-tuple-element.6.refs_0_, bf16[2,400,512]{2,1,0:T(8,128)(2,1)} %get-tuple-element.7.refs_1_, bf16[2,400,512]{2,1,0:T(8,128)(2,1)} %get-tuple-element.8.refs_2_), custom_call_target="tpu_custom_call" | custom-call | tf_op jit(solution)/shard_map/pallas_call | solution.py:389
